TPU v7x, 256 devices: a whole 4x4x8 slice. The times are simulated.
256 devices in a mesh: group: 8 (over x, core), sub: 32 (over y, z).
Axes of the slice: x: 4, y: 4, z: 8, core: 2. Of those that a mesh axis runs over, the one named last changes fastest.
Arguments:
- resid_iface: float32 [256, 16, 4352], P(('group', 'sub')), may hold values from -6 to 6
- resid_inner: float32 [256, 16, 3072], P(('group', 'sub')), may hold values from -6 to 6
- weights: float32 [256, 4352], P(('group', 'sub')), may hold values from 0.25 to 0.75
- nbr: int32 [256, 32], P(('group', 'sub')), may hold values from 0 to 1, as said below
- own2: int32 [256, 128], P(('group', 'sub')), may hold values from 0 to 2047
- cidx: int32 [256, 8], P(('group', 'sub')), may hold values from 0 to 16
- neumann: bfloat16 [256, 17, 256, 256], P(('group', 'sub'))
- dirichlet: bfloat16 [256, 8, 384, 384], P(('group', 'sub'))
- coupling: bfloat16 [256, 8, 256, 384], P(('group', 'sub')), may hold values from -0.375 to 0.375
- coarse_basis: bfloat16 [256, 4352, 128], P(('group', 'sub')), may hold values from -0.5 to 0.5
- group_basis: float32 [16384, 512], P(('group', 'sub')), may hold values from -0.25 to 0.25
- group_inverse: float32 [16384, 2048], P('group', 'sub'), as said below
- top_inverse: float32 [512, 512], replicated, as said below
Outputs:
- interface_out: float32 [256, 16, 4352], P(('group', 'sub'))
- interior_out: float32 [256, 16, 3072], P(('group', 'sub'))
Inputs may be any that keep to these rules, and one draw needn't show every extreme that they name: Symmetric within each group (nbr[(g, q), j] = nbr[(g, j), q]) with nbr[(g, q), q] = 0. `group_inverse`: each matrix of a group is symmetric. `top_inverse`: symmetric.
All inputs are finite; a program needn't handle non-finite values.
Results may differ from a plain program's by a relative error of at most 0.013.
Values may be sent and summed in bfloat16 or wider, within the bound.
A program may use at most 64 MiB of HBM per device.

v0:
```python
import jax
import jax.numpy as jnp
from jax import lax
from jax.sharding import PartitionSpec as P


def padded_2(cells, sides, width):
    for axis, dim in sides:
        count = lax.axis_size(axis)
        ends = count - 1
        head = lax.slice_in_dim(cells, 0, width, axis=dim)
        tail = lax.slice_in_dim(cells, cells.shape[dim] - width, cells.shape[dim], axis=dim)
        cells = jnp.concatenate(
            [
                lax.ppermute(tail, axis, [(i, (i + 1) % count) for i in range(ends)]),
                cells,
                lax.ppermute(head, axis, [((i + 1) % count, i) for i in range(ends)]),
            ],
            axis=dim,
        )
    return cells


def shards(
    resid_iface,
    resid_inner,
    weights,
    nbr,
    own2,
    cidx,
    neumann,
    dirichlet,
    coupling,
    coarse_basis,
    group_basis,
    group_inverse,
    top_inverse,
):
    highest = lax.Precision.HIGHEST
    nsub = lax.axis_size("sub")
    mine = lax.axis_index("sub")
    rows = resid_iface.shape[1]
    width = resid_iface.shape[2]
    slot_width = width // (nsub + 2)
    block_count = neumann.shape[1]
    block_width = neumann.shape[2]
    inner_count = dirichlet.shape[1]
    inner_width = dirichlet.shape[2]
    group_width = group_inverse.shape[0]
    share = group_inverse.shape[1]
    slot_mask = jnp.concatenate([nbr[0].astype(jnp.float32), jnp.ones((2,), jnp.float32)])
    scale = jnp.repeat(slot_mask, slot_width) * weights[0]
    weighted = (scale[None, :] * resid_iface[0]).astype(jnp.bfloat16)
    local0 = jnp.dot(weighted, coarse_basis[0], preferred_element_type=jnp.float32)
    onehot = (own2[0][:, None] == jnp.arange(group_width, dtype=jnp.int32)[None, :]).astype(
        jnp.float32
    )
    contrib = jnp.dot(local0, onehot, precision=highest)
    level2 = lax.psum(contrib.astype(jnp.bfloat16), "sub").astype(jnp.float32)
    level2_mine = lax.dynamic_slice_in_dim(level2, mine * share, share, 1)
    neumann_part = jnp.einsum(
        "rkb,kbc->rkc",
        weighted.reshape(rows, block_count, block_width),
        neumann[0],
        preferred_element_type=jnp.float32,
    ).reshape(rows, width)
    top_term = jnp.dot(level2_mine, group_basis, precision=highest)
    level3 = lax.psum(top_term, ("group", "sub"))
    coarse3 = jnp.dot(level3, top_inverse, precision=highest)
    lifted = lax.dot_general(coarse3, group_basis, (((1,), (1,)), ((), ())), precision=highest)
    coarse2_mine = jnp.dot(level2, group_inverse, precision=highest) + lifted
    coarse2 = lax.all_gather(coarse2_mine.astype(jnp.bfloat16), "sub", axis=1, tiled=True)
    values = jnp.take(coarse2, own2[0], axis=1)
    spread = lax.dot_general(
        values, coarse_basis[0], (((1,), (1,)), ((), ())), preferred_element_type=jnp.float32
    )
    scaled = scale[None, :] * (neumann_part + spread)
    slots = scaled.reshape(rows, nsub + 2, slot_width)
    received = lax.all_to_all(
        slots[:, :nsub, :].astype(jnp.bfloat16), "sub", split_axis=1, concat_axis=1, tiled=True
    ).astype(jnp.float32)
    padded = padded_2(slots[:, nsub:, :], (("group", 1),), 1)
    lower_face = slots[:, nsub, :] + padded[:, 0, :]
    upper_face = slots[:, nsub + 1, :] + padded[:, 3, :]
    total = jnp.concatenate(
        [slots[:, :nsub, :] + received, lower_face[:, None, :], upper_face[:, None, :]], axis=1
    )
    interface_out = total.reshape(rows, width)
    iface_blocks = interface_out.reshape(rows, block_count, block_width).astype(jnp.bfloat16)
    picked = jnp.take(iface_blocks, cidx[0], axis=1)
    pushed = jnp.einsum("rkb,kbc->rkc", picked, coupling[0], preferred_element_type=jnp.float32)
    inner_rhs = (resid_inner[0].reshape(rows, inner_count, inner_width) - pushed).astype(
        jnp.bfloat16
    )
    interior_out = jnp.einsum(
        "rkb,kbc->rkc", inner_rhs, dirichlet[0], preferred_element_type=jnp.float32
    ).reshape(rows, inner_count * inner_width)
    return (interface_out[None], interior_out[None])


def solution(mesh):
    placed = (
        P(("group", "sub"), None, None),
        P(("group", "sub"), None, None),
        P(("group", "sub"), None),
        P(("group", "sub"), None),
        P(("group", "sub"), None),
        P(("group", "sub"), None),
        P(("group", "sub"), None, None, None),
        P(("group", "sub"), None, None, None),
        P(("group", "sub"), None, None, None),
        P(("group", "sub"), None, None),
        P(("group", "sub"), None),
        P("group", "sub"),
        P(),
    )
    return jax.shard_map(
        shards,
        mesh=mesh,
        in_specs=placed,
        out_specs=(P(("group", "sub"), None, None), P(("group", "sub"), None, None)),
        check_vma=False,
    )
```

profile of v0, /device:TPU:1, one launch (start us, length us, event | category | flops | bytes accessed | tf_op | source)
XLA Modules:
  0.0 318.7 jit_solution(4623421728509135453)
XLA Ops:
  7.2 0.0 all-reduce.3.cloned.1.call-start
  7.3 0.8 convert_bitcast_fusion
  8.1 0.1 broadcast_bitcast_fusion
  8.1 0.8 fusion.45
  8.9 1.6 fusion.25
  10.5 1.8 convolution_convert_fusion
  12.3 0.0 all-reduce.3.cloned.1.call-update
  12.6 2.0 fusion.7
  14.6 0.7 copy.43
  15.3 136.0 %all-reduce.3.cloned.1.call-done = bf16[16,2048]{1,0:T(8,128)(2,1)} async-done(((bf16[16,2048]{1,0:T(8,128)(2,1)}), bf16[16,2048]{1,0:T(8,128)(2,1)}) %all-reduce.3.cloned.1.call-update) | async-done | bytes 65552 | tf_op jit(solution)/shard_map/psum | solution.py:59
  151.3 1.7 fusion.47
  153.0 78.0 %psum.15 = f32[16,512]{1,0:T(8,128)S(1)} all-reduce(f32[16,512]{1,0:T(8,128)} %fusion.47), channel_id=1, replica_groups=mesh['group'=8,'sub'=32] {'group','sub'}, use_global_device_ids=true, to_apply=%region_1.0 | all-reduce | flops 8192 | bytes 65536 | tf_op jit(solution)/shard_map/psum | solution.py:68
  231.1 1.9 fusion.58
  233.0 1.4 fusion.57
  234.4 0.2 fusion.28
  234.6 35.0 %all-gather = bf16[32,64,16]{1,2,0:T(8,128)(2,1)} all-gather(bf16[1,64,16]{1,2,0:T(8,128)(2,1)S(1)} %fusion.28), channel_id=1, replica_groups=mesh['group'=8,'sub'=32] {'sub'}, dimensions={0}, use_global_device_ids=true | all-gather | bytes 67584 | tf_op jit(solution)/shard_map/all_gather | solution.py:72
  269.6 1.9 copy.41
  271.5 1.8 gather_fusion
  273.3 2.2 fusion
  275.5 1.0 reshape.101
  276.5 12.7 %collective-permute-start = (f32[16,1,128]{2,1,0:T(1,128)S(1)}, f32[16,1,128]{2,1,0:T(1,128)S(1)}, u32[]{:S(2)}, u32[]{:S(2)}) collective-permute-start(f32[16,1,128]{2,1,0:T(1,128)S(1)} %get-tuple-element.4), channel_id=1, source_target_pairs={{0,32},{32,64},{64,96},{96,128},{128,160},{160,192},{192,224},{1,3... | collective-permute-start | bytes 24584 | tf_op jit(solution)/shard_map/ppermute | solution.py:15
  289.2 1.9 collective-permute-start.1
  291.2 0.7 copy.36
  291.9 5.6 %all-to-all-start = ((bf16[16,32,128]{2,0,1:T(8,128)(2,1)}), bf16[16,32,128]{2,0,1:T(8,128)(2,1)S(1)}, u32[]{:S(2)}, u32[]{:S(2)}) async-start(bf16[16,32,128]{2,0,1:T(8,128)(2,1)} %copy.36), calls=%async_computation | async-start | bytes 262144 | tf_op jit(solution)/shard_map/all_to_all | solution.py:79
  297.5 1.0 copy.45
  298.6 8.8 %all-to-all-done = bf16[16,32,128]{2,0,1:T(8,128)(2,1)S(1)} async-done(((bf16[16,32,128]{2,0,1:T(8,128)(2,1)}), bf16[16,32,128]{2,0,1:T(8,128)(2,1)S(1)}, u32[]{:S(2)}, u32[]{:S(2)}) %all-to-all-start) | async-done | bytes 131104 | tf_op jit(solution)/shard_map/all_to_all | solution.py:79
  307.5 0.1 convert_element_type.48
  307.6 0.6 gather_fusion.1
  308.2 2.1 fusion.10
  310.3 0.1 copy.40
  310.4 0.7 broadcast_in_dim_reshape.7
  311.1 0.8 broadcast_in_dim_reshape.6
  (31 shorter events, 0.4 us)
Async XLA Ops:
  7.2 301.0 %copy-start = (bf16[1,8,384,384]{3,2,1,0:T(8,128)(2,1)S(1)}, bf16[1,8,384,384]{3,2,1,0:T(8,128)(2,1)}, u32[]{:S(2)}) copy-start(bf16[1,8,384,384]{3,2,1,0:T(8,128)(2,1)} %param.20) | copy-start | bytes 7077892
  7.2 5.2 %copy-start.2 = (f32[1,16,4352]{2,1,0:T(8,128)S(1)}, f32[1,16,4352]{2,1,0:T(8,128)}, u32[]{:S(2)}) copy-start(f32[1,16,4352]{2,1,0:T(8,128)} %param.13) | copy-start | bytes 835588
  7.2 5.2 %copy-start.4 = (s32[1,128]{1,0:T(1,128)S(1)}, s32[1,128]{1,0:T(1,128)}, u32[]{:S(2)}) copy-start(s32[1,128]{1,0:T(1,128)} %param.17) | copy-start | bytes 1540
  7.2 5.3 %copy-start.5 = (s32[1,8]{1,0:T(1,128)S(1)}, s32[1,8]{1,0:T(1,128)}, u32[]{:S(2)}) copy-start(s32[1,8]{1,0:T(1,128)} %param.18) | copy-start | bytes 100
  7.2 144.1 %all-reduce.3.cloned.1.call-start = ((), (), s32[]{:S(2)}) async-start(), calls=%async_computation.1 | async-start | bytes 131072 | tf_op jit(solution)/shard_map/psum | solution.py:59
  15.3 257.9 %copy-start.1 = (bf16[1,4352,128]{2,1,0:T(8,128)(2,1)S(1)}, bf16[1,4352,128]{2,1,0:T(8,128)(2,1)}, u32[]{:S(2)}) copy-start(bf16[1,4352,128]{2,1,0:T(8,128)(2,1)} %param.22) | copy-start | bytes 3342340
  231.1 3.3 %copy-start.3 = (f32[64,512]{1,0:T(8,128)S(1)}, f32[64,512]{1,0:T(8,128)}, u32[]{:S(2)}) copy-start(f32[64,512]{1,0:T(8,128)} %param.23) | copy-start | bytes 393220
  276.5 22.0 %collective-permute-start = (f32[16,1,128]{2,1,0:T(1,128)S(1)}, f32[16,1,128]{2,1,0:T(1,128)S(1)}, u32[]{:S(2)}, u32[]{:S(2)}) collective-permute-start(f32[16,1,128]{2,1,0:T(1,128)S(1)} %get-tuple-element.4), channel_id=1, source_target_pairs={{0,32},{32,64},{64,96},{96,128},{128,160},{160,192},{192,224},{1,3... | collective-permute-start | bytes 24584 | tf_op jit(solution)/shard_map/ppermute | solution.py:15
  289.2 9.3 %collective-permute-start.1 = (f32[16,1,128]{2,1,0:T(1,128)S(1)}, f32[16,1,128]{2,1,0:T(1,128)S(1)}, u32[]{:S(2)}, u32[]{:S(2)}) collective-permute-start(f32[16,1,128]{2,1,0:T(1,128)S(1)} %get-tuple-element.5), channel_id=1, source_target_pairs={{32,0},{64,32},{96,64},{128,96},{160,128},{192,160},{224,192},{33,... | collective-permute-start | bytes 24584 | tf_op jit(solution)/shard_map/ppermute | solution.py:17
  291.9 15.5 %all-to-all-start = ((bf16[16,32,128]{2,0,1:T(8,128)(2,1)}), bf16[16,32,128]{2,0,1:T(8,128)(2,1)S(1)}, u32[]{:S(2)}, u32[]{:S(2)}) async-start(bf16[16,32,128]{2,0,1:T(8,128)(2,1)} %copy.36), calls=%async_computation | async-start | bytes 262144 | tf_op jit(solution)/shard_map/all_to_all | solution.py:79
Sparse Core Ops, SparseCore 0:
  12.5 138.7 all-reduce.2
where the time goes:
time: 319 us
  waiting for transfers between devices  145 us (45%)
  blocking collectives  113 us (35%)
  starting transfers between devices  20.3 us (6%)
  matrix products  15 us (5%)
  between operations  14.3 us (4%)
  local copies, waits for them, and re-layouts  9.48 us (3%)
    psum x1, waiting for transfers between devices, shards(): level2 = lax.psum(contrib.astype(jnp.bfloat16), 'sub').astype(jnp.float32)  136 us
    psum x1, blocking collectives, shards(): level3 = lax.psum(top_term, ('group', 'sub'))  78 us
    all_gather x1, blocking collectives, shards(): lax.all_gather(coarse2_mine.astype(jnp.bfloat16), 'sub', axis=1, tiled=True)  35 us
    ppermute x1, starting transfers between devices, padded_2(): lax.ppermute(tail, axis, [(i, (i + 1) % count) for i in range(ends)])  12.7 us
    all_to_all x1, waiting for transfers between devices, shards(): lax.all_to_all(slots[:, :nsub, :].astype(jnp.bfloat16), 'sub', split_axis...  8.85 us
  transfers between devices with their start and end apart: 4, of which 2 were waited for; matrix products, arithmetic and copies ran while one was open for 1% of the time, Pallas kernels for 0%

commit v1 on v0

--- a/solution.py
+++ b/solution.py
@@ -69,7 +69,11 @@
     coarse3 = jnp.dot(level3, top_inverse, precision=highest)
     lifted = lax.dot_general(coarse3, group_basis, (((1,), (1,)), ((), ())), precision=highest)
     coarse2_mine = jnp.dot(level2, group_inverse, precision=highest) + lifted
-    coarse2 = lax.all_gather(coarse2_mine.astype(jnp.bfloat16), "sub", axis=1, tiled=True)
+    x = coarse2_mine.astype(jnp.bfloat16)
+    size = lax.axis_size("sub")
+    blocks = jnp.stack([x for _ in range(size)])
+    blocks = lax.all_to_all(blocks, "sub", split_axis=0, concat_axis=0)
+    coarse2 = jnp.concatenate(blocks, axis=1)
     values = jnp.take(coarse2, own2[0], axis=1)
     spread = lax.dot_general(
         values, coarse_basis[0], (((1,), (1,)), ((), ())), preferred_element_type=jnp.float32

time: 319 us -> 292 us (0.915)
  blocking collectives: 113 us -> 78 us
  waiting for transfers between devices: 145 us -> 152 us
  local copies, waits for them, and re-layouts: 9.48 us -> 14.5 us
  starting transfers between devices: 20.3 us -> 16.5 us
    all_gather x1 -> x0, blocking collectives: 35 us -> none  [shards(): lax.all_gather(coarse2_mine.astype(jnp.bfloat16), 'sub', axis=1, tiled=True)]
    ppermute x1, starting transfers between devices: 12.7 us -> 4.14 us  [padded_2(): lax.ppermute(tail, axis, [(i, (i + 1) % count) for i in range(ends)])]
    all_to_all x0 -> x1, waiting for transfers between devices: none -> 7.13 us  [shards(): blocks = lax.all_to_all(blocks, 'sub', split_axis=0, concat_axis=0)]
    all_to_all x0 -> x1, starting transfers between devices: none -> 6.54 us  [shards(): blocks = lax.all_to_all(blocks, 'sub', split_axis=0, concat_axis=0)]
  transfers between devices with their start and end apart: 4 -> 5, of which waited for: 2 -> 3; matrix products, arithmetic and copies ran while one was open for 1% -> 2% of each run, Pallas kernels for 0% -> 0%
where the time goes in v1:
time: 292 us; the launch traced here: 291 us
  waiting for transfers between devices  152 us (52%)
  blocking collectives  78 us (27%)
  starting transfers between devices  16.5 us (6%)
  local copies, waits for them, and re-layouts  14.5 us (5%)
  matrix products  14.4 us (5%)
  between operations  14.3 us (5%)
    psum x1, waiting for transfers between devices, shards(): level2 = lax.psum(contrib.astype(jnp.bfloat16), 'sub').astype(jnp.float32)  136 us
    psum x1, blocking collectives, shards(): level3 = lax.psum(top_term, ('group', 'sub'))  78 us
    all_to_all x1, waiting for transfers between devices, shards(): lax.all_to_all(slots[:, :nsub, :].astype(jnp.bfloat16), 'sub', split_axis...  8.63 us
    all_to_all x1, waiting for transfers between devices, shards(): blocks = lax.all_to_all(blocks, 'sub', split_axis=0, concat_axis=0)  7.13 us
    all_to_all x1, starting transfers between devices, shards(): blocks = lax.all_to_all(blocks, 'sub', split_axis=0, concat_axis=0)  6.54 us
  transfers between devices with their start and end apart: 5, of which 3 were waited for; matrix products, arithmetic and copies ran while one was open for 2% of the time, Pallas kernels for 0%

profile of v1, /device:TPU:1, one launch (start us, length us, event | category | flops | bytes accessed | tf_op | source)
XLA Modules:
  0.0 291.2 jit_solution(15601048837408812498)
XLA Ops:
  7.2 0.8 convert_bitcast_fusion
  8.1 0.8 fusion.44
  8.9 1.6 fusion.25
  10.5 1.8 convolution_convert_fusion
  12.6 2.8 fusion.7
  15.4 135.9 %all-reduce.3.cloned.1.call-done = bf16[16,2048]{1,0:T(8,128)(2,1)} async-done(((bf16[16,2048]{1,0:T(8,128)(2,1)}), bf16[16,2048]{1,0:T(8,128)(2,1)}) %all-reduce.3.cloned.1.call-update) | async-done | bytes 65552 | tf_op jit(solution)/shard_map/psum | solution.py:59
  151.3 1.5 fusion.46
  152.8 78.0 %psum.15 = f32[16,512]{1,0:T(8,128)S(1)} all-reduce(f32[16,512]{1,0:T(8,128)} %fusion.46), channel_id=1, replica_groups=mesh['group'=8,'sub'=32] {'group','sub'}, use_global_device_ids=true, to_apply=%region_1.0 | all-reduce | flops 8192 | bytes 65536 | tf_op jit(solution)/shard_map/psum | solution.py:68
  230.9 0.6 fusion.57
  231.5 1.5 fusion.56
  233.0 0.2 fusion.27
  233.2 0.7 stack.2
  233.9 1.7 reshape.130
  235.6 6.5 %all-to-all-start = ((bf16[32,2,512]{2,1,0:T(2,128)(2,1)}), bf16[32,2,512]{2,1,0:T(2,128)(2,1)}, u32[]{:S(2)}, u32[]{:S(2)}) async-start(bf16[32,2,512]{2,1,0:T(2,128)(2,1)} %reshape.130), calls=%async_computation | async-start | bytes 131072 | tf_op jit(solution)/shard_map/all_to_all | solution.py:75
  242.1 1.7 copy.39
  243.8 7.1 %all-to-all-done = bf16[32,2,512]{2,1,0:T(2,128)(2,1)} async-done(((bf16[32,2,512]{2,1,0:T(2,128)(2,1)}), bf16[32,2,512]{2,1,0:T(2,128)(2,1)}, u32[]{:S(2)}, u32[]{:S(2)}) %all-to-all-start) | async-done | bytes 65568 | tf_op jit(solution)/shard_map/all_to_all | solution.py:75
  251.0 1.7 reshape.131
  252.6 1.9 copy.33
  254.5 1.8 gather_fusion
  256.3 2.2 fusion
  258.5 1.0 reshape.111
  259.6 4.1 %collective-permute-start = (f32[16,1,128]{2,1,0:T(1,128)S(1)}, f32[16,1,128]{2,1,0:T(1,128)S(1)}, u32[]{:S(2)}, u32[]{:S(2)}) collective-permute-start(f32[16,1,128]{2,1,0:T(1,128)S(1)} %get-tuple-element.4), channel_id=1, source_target_pairs={{0,32},{32,64},{64,96},{96,128},{128,160},{160,192},{192,224},{1,3... | collective-permute-start | bytes 24584 | tf_op jit(solution)/shard_map/ppermute | solution.py:15
  263.7 1.9 collective-permute-start.1
  265.6 0.7 copy.34
  266.3 3.9 %all-to-all-start.1 = ((bf16[16,32,128]{2,0,1:T(8,128)(2,1)}), bf16[16,32,128]{2,0,1:T(8,128)(2,1)S(1)}, u32[]{:S(2)}, u32[]{:S(2)}) async-start(bf16[16,32,128]{2,0,1:T(8,128)(2,1)} %copy.34), calls=%async_computation.1 | async-start | bytes 262144 | tf_op jit(solution)/shard_map/all_to_all | solution.py:83
  270.2 1.0 copy.41
  271.2 8.6 %all-to-all-done.1 = bf16[16,32,128]{2,0,1:T(8,128)(2,1)S(1)} async-done(((bf16[16,32,128]{2,0,1:T(8,128)(2,1)}), bf16[16,32,128]{2,0,1:T(8,128)(2,1)S(1)}, u32[]{:S(2)}, u32[]{:S(2)}) %all-to-all-start.1) | async-done | bytes 131104 | tf_op jit(solution)/shard_map/all_to_all | solution.py:83
  280.1 0.6 gather_fusion.1
  280.7 2.1 fusion.10
  282.8 0.1 copy.38
  282.9 0.7 broadcast_in_dim_reshape.7
  283.6 0.8 broadcast_in_dim_reshape.6
  (43 shorter events, 0.6 us)
Async XLA Ops:
  7.2 273.5 %copy-start = (bf16[1,8,384,384]{3,2,1,0:T(8,128)(2,1)S(1)}, bf16[1,8,384,384]{3,2,1,0:T(8,128)(2,1)}, u32[]{:S(2)}) copy-start(bf16[1,8,384,384]{3,2,1,0:T(8,128)(2,1)} %param.20) | copy-start | bytes 7077892
  7.2 5.2 %copy-start.2 = (f32[1,16,4352]{2,1,0:T(8,128)S(1)}, f32[1,16,4352]{2,1,0:T(8,128)}, u32[]{:S(2)}) copy-start(f32[1,16,4352]{2,1,0:T(8,128)} %param.13) | copy-start | bytes 835588
  7.2 5.2 %copy-start.8 = (s32[1,128]{1,0:T(1,128)S(1)}, s32[1,128]{1,0:T(1,128)}, u32[]{:S(2)}) copy-start(s32[1,128]{1,0:T(1,128)} %param.17) | copy-start | bytes 1540
  7.2 144.1 %all-reduce.3.cloned.1.call-start = ((), (), s32[]{:S(2)}) async-start(), calls=%async_computation.2 | async-start | bytes 131072 | tf_op jit(solution)/shard_map/psum | solution.py:59
  8.9 3.5 %copy-start.6 = (f32[4352]{0:T(1024)}, f32[4352]{0:T(1024)S(1)}, u32[]{:S(2)}) copy-start(f32[4352]{0:T(1024)S(1)} %fusion.44) | copy-start | bytes 52228
  12.5 2.9 %copy-start.9 = (s32[1,8]{1,0:T(1,128)S(1)}, s32[1,8]{1,0:T(1,128)}, u32[]{:S(2)}) copy-start(s32[1,8]{1,0:T(1,128)} %param.18) | copy-start | bytes 100
  12.5 138.8 %copy-start.4 = (f32[64,512]{1,0:T(8,128)S(1)}, f32[64,512]{1,0:T(8,128)}, u32[]{:S(2)}) copy-start(f32[64,512]{1,0:T(8,128)} %param.23) | copy-start | bytes 393220
  12.5 218.3 %copy-start.3 = (f32[512,512]{1,0:T(8,128)S(1)}, f32[512,512]{1,0:T(8,128)}, u32[]{:S(2)}) copy-start(f32[512,512]{1,0:T(8,128)} %param.25) | copy-start | bytes 3145732
  230.9 2.1 copy-start.5
  231.5 24.8 %copy-start.1 = (bf16[1,4352,128]{2,1,0:T(8,128)(2,1)S(1)}, bf16[1,4352,128]{2,1,0:T(8,128)(2,1)}, u32[]{:S(2)}) copy-start(bf16[1,4352,128]{2,1,0:T(8,128)(2,1)} %param.22) | copy-start | bytes 3342340
  231.5 24.8 %copy-start.7 = (f32[4352]{0:T(1024)S(1)}, f32[4352]{0:T(1024)}, u32[]{:S(2)}) copy-start(f32[4352]{0:T(1024)} %copy-done.6) | copy-start | bytes 52228
  235.6 15.4 %all-to-all-start = ((bf16[32,2,512]{2,1,0:T(2,128)(2,1)}), bf16[32,2,512]{2,1,0:T(2,128)(2,1)}, u32[]{:S(2)}, u32[]{:S(2)}) async-start(bf16[32,2,512]{2,1,0:T(2,128)(2,1)} %reshape.130), calls=%async_computation | async-start | bytes 131072 | tf_op jit(solution)/shard_map/all_to_all | solution.py:75
  259.6 11.6 %collective-permute-start = (f32[16,1,128]{2,1,0:T(1,128)S(1)}, f32[16,1,128]{2,1,0:T(1,128)S(1)}, u32[]{:S(2)}, u32[]{:S(2)}) collective-permute-start(f32[16,1,128]{2,1,0:T(1,128)S(1)} %get-tuple-element.4), channel_id=1, source_target_pairs={{0,32},{32,64},{64,96},{96,128},{128,160},{160,192},{192,224},{1,3... | collective-permute-start | bytes 24584 | tf_op jit(solution)/shard_map/ppermute | solution.py:15
  263.7 7.5 %collective-permute-start.1 = (f32[16,1,128]{2,1,0:T(1,128)S(1)}, f32[16,1,128]{2,1,0:T(1,128)S(1)}, u32[]{:S(2)}, u32[]{:S(2)}) collective-permute-start(f32[16,1,128]{2,1,0:T(1,128)S(1)} %get-tuple-element.5), channel_id=1, source_target_pairs={{32,0},{64,32},{96,64},{128,96},{160,128},{192,160},{224,192},{33,... | collective-permute-start | bytes 24584 | tf_op jit(solution)/shard_map/ppermute | solution.py:17
  266.3 13.5 %all-to-all-start.1 = ((bf16[16,32,128]{2,0,1:T(8,128)(2,1)}), bf16[16,32,128]{2,0,1:T(8,128)(2,1)S(1)}, u32[]{:S(2)}, u32[]{:S(2)}) async-start(bf16[16,32,128]{2,0,1:T(8,128)(2,1)} %copy.34), calls=%async_computation.1 | async-start | bytes 262144 | tf_op jit(solution)/shard_map/all_to_all | solution.py:83
Sparse Core Ops, SparseCore 0:
  12.5 138.7 all-reduce.2
